TPU v7x, 32 devices: a whole 2x2x4 slice. The times are simulated.
32 devices in a mesh: section: 4 (over y, x), seq: 2 (over core), dp: 4 (over z).
Axes of the slice: x: 2, y: 2, z: 4, core: 2. Of those that a mesh axis runs over, the one named last changes fastest.
Arguments:
- bases: int32 [8, 3072, 128], P('dp', 'seq'), may hold values from 0 to 3
- targets: int32 [8, 3072, 4096], P('dp', 'seq', 'section'), may hold values from 0 to 2
- stem_weight: bfloat16 [512, 384], replicated, may hold values from -0.5 to 0.5
- conv_weight: bfloat16 [4, 3, 384, 192], P('section'), may hold values from -0.1875 to 0.1875
- proj_weight: bfloat16 [4, 192, 384], P('section'), may hold values from -0.4375 to 0.4375
- head_weight: bfloat16 [384, 4096], P(None, 'section'), may hold values from -0.078125 to 0.078125
Outputs:
- conv_grad: float32 [4, 3, 384, 192], P('section')
- proj_grad: float32 [4, 192, 384], P('section')
- head_grad: float32 [384, 4096], P(None, 'section')
All inputs are finite; a program needn't handle non-finite values.
Results may differ from a plain program's by a relative error of at most 0.0014.
Values may be sent and summed in bfloat16 or wider, within the bound.
A program may use at most 128 MiB of HBM per device.

v0:
```python
import math

import jax
import jax.numpy as jnp
from jax import lax
from jax.experimental import pallas as pl
from jax.experimental.pallas import tpu as pltpu
from jax.sharding import PartitionSpec as P

SQRT_TWO_OVER_PI = 0.7978845608028654
CUBIC_TERM = 0.044715


def gelu_value(inputs):
    return (
        0.5
        * inputs
        * (1.0 + jnp.tanh(SQRT_TWO_OVER_PI * (inputs + CUBIC_TERM * inputs * inputs * inputs)))
    )


def gelu_slope(inputs):
    tangent = jnp.tanh(SQRT_TWO_OVER_PI * (inputs + CUBIC_TERM * inputs * inputs * inputs))
    return 0.5 * (1.0 + tangent) + 0.5 * inputs * (1.0 - tangent * tangent) * SQRT_TWO_OVER_PI * (
        1.0 + 3.0 * CUBIC_TERM * inputs * inputs
    )


def contract_rows(left_side, right_side):
    return lax.dot_general(
        left_side, right_side, (((0,), (0,)), ((), ())), preferred_element_type=jnp.float32
    )


def times_transposed(left_side, right_side):
    return lax.dot_general(
        left_side, right_side, (((1,), (1,)), ((), ())), preferred_element_type=jnp.float32
    )


def shift_rows(value, by):
    if abs(by) >= value.shape[0]:
        return jnp.zeros_like(value)
    pad = jnp.zeros((abs(by),) + value.shape[1:], value.dtype)
    if by > 0:
        return jnp.concatenate([pad, value[:-by]], 0)
    return jnp.concatenate([value[-by:], pad], 0)


MESH = pl.DeviceIdType.MESH
ANY = pl.BlockSpec(memory_space=pl.ANY)


def greet(peers):
    barrier = pltpu.get_barrier_semaphore()
    for peer in peers:
        pl.semaphore_signal(barrier, inc=1, device_id=peer, device_id_type=MESH)
    pl.semaphore_wait(barrier, len(peers))


def remote(src, dst, send, recv, peer):
    return pltpu.make_async_remote_copy(
        src_ref=src, dst_ref=dst, send_sem=send, recv_sem=recv, device_id=peer, device_id_type=MESH
    )


def both_gelu(inputs):
    square = inputs * inputs
    tangent = jnp.tanh(
        inputs * (SQRT_TWO_OVER_PI + (SQRT_TWO_OVER_PI * CUBIC_TERM) * square)
    )
    gate = 0.5 + 0.5 * tangent
    value = inputs * gate
    inside = 2.0 * SQRT_TWO_OVER_PI + (6.0 * SQRT_TWO_OVER_PI * CUBIC_TERM) * square
    return value, gate + value * (1.0 - gate) * inside


def tile_of(rows):
    for size in (512, 384, 256, 192, 128, 96, 64, 48, 32, 16):
        if rows % size == 0:
            return size
    return rows


def forward_tower(bases, stem, taps, proj, sections, unit):
    seqs, half, width = bases.shape
    length = seqs * half
    channels = stem.shape[1]
    inner = proj.shape[0]
    rows = taps.shape[0] + inner
    part = rows // 2
    tile = tile_of(half)
    steps = half // tile
    team = 3 if steps % 3 == 0 else 1
    shifts = [unit * 2**k for k in range(sections)]

    def kernel(*refs):
        bases_ref, stem_ref, taps_ref, proj_ref = refs[:4]
        refs = refs[4:]
        top_ref, weights_ref = refs[:2]
        hidden_out, slope_out = refs[2 : 2 + sections], refs[2 + sections : 1 + 2 * sections]
        refs = refs[1 + 2 * sections :]
        active_out, bend_out = refs[:sections], refs[sections : 2 * sections]
        refs = refs[2 * sections :]
        full, held, turned, state = refs[:4]
        refs = refs[4:]
        hidden, slope = refs[:sections], refs[sections : 2 * sections - 1]
        refs = refs[2 * sections - 1 :]
        active, bend = refs[:sections], refs[sections : 2 * sections]
        refs = refs[2 * sections :]
        bsend, brecv, send, recv, send2, recv2, tsend, trecv, own_sem, out_sem = refs

        s, c = lax.axis_index("section"), lax.axis_index("seq")
        partner = {"section": s, "seq": 1 - c}
        peers = [{"section": lax.rem(s + k, sections), "seq": c} for k in range(1, sections)]
        loads = [
            pltpu.make_async_copy(bases_ref.at[c], full.at[c], own_sem.at[0]),
            pltpu.make_async_copy(
                taps_ref, held.at[s, pl.ds(0, taps.shape[0])], own_sem.at[1]
            ),
            pltpu.make_async_copy(
                proj_ref, held.at[s, pl.ds(taps.shape[0], inner)], own_sem.at[2]
            ),
        ]
        for copy in loads:
            copy.start()
        greet(peers + [partner])
        across = remote(bases_ref.at[1 - c], full.at[c], bsend, brecv, partner)
        across.start()
        loads[1].wait()
        loads[2].wait()
        mine = held.at[s, pl.ds(pl.multiple_of(c * part, 16), part)]
        first = []
        for k, peer in enumerate(peers):
            first.append(remote(mine, mine, send.at[k], recv.at[k], peer))
            first[-1].start()
        for k in range(sections):
            edge = jnp.zeros((shifts[k], channels), jnp.bfloat16)
            hidden[k][pl.ds(0, shifts[k]), :] = edge
            hidden[k][pl.ds(shifts[k] + length, shifts[k]), :] = edge

        def begin(number):
            def step(i, carry):
                at = i * tile
                codes = full[number, pl.ds(pl.multiple_of(at, 16), tile), :]
                onehot = jnp.concatenate(
                    [(codes == k).astype(jnp.bfloat16) for k in range(4)], 1
                )
                start = jnp.dot(onehot, stem_ref[...], preferred_element_type=jnp.float32)
                start = start.astype(jnp.bfloat16)
                place = pl.multiple_of(number * half + at, 16)
                state[pl.ds(place, tile), :] = start
                value = gelu_value(start.astype(jnp.float32)).astype(jnp.bfloat16)
                hidden[0][pl.ds(pl.multiple_of(shifts[0] + place, 16), tile), :] = value
                return carry

            lax.fori_loop(0, steps, step, 0)

        loads[0].wait()
        begin(c)
        across.wait_recv()
        begin(1 - c)

        second = []
        for k in range(sections - 1):
            first[k].wait_recv()
            source = lax.rem(s + sections - 1 - k, sections)
            piece = held.at[source, pl.ds(pl.multiple_of(c * part, 16), part)]
            second.append(remote(piece, piece, send2.at[k], recv2.at[k], partner))
            second[-1].start()
        for copy in second:
            copy.wait_recv()

        outs = []

        def keep(src, dst):
            outs.append(pltpu.make_async_copy(src, dst, out_sem.at[len(outs)]))
            outs[-1].start()

        keep(held, weights_ref)
        keep(hidden[0].at[pl.ds(shifts[0], length)], hidden_out[0])

        for k in range(sections):
            by = shifts[k]
            for j in range(3):
                tap = held[k, pl.ds(j * inner, inner), :]
                turned[pl.ds(j * channels, channels), :] = tap.T

            def group(places, k=k, by=by):
                inners = []
                for place in places:
                    wide = jnp.concatenate(
                        [
                            hidden[k][pl.ds(pl.multiple_of(place + j * by, 16), tile), :]
                            for j in range(3)
                        ],
                        1,
                    )
                    inners.append(
                        jnp.dot(wide, turned[...], preferred_element_type=jnp.float32)
                    )
                olds = [state[pl.ds(place, tile), :].astype(jnp.float32) for place in places]
                results = []
                for inner_sum, old in zip(inners, olds):
                    value, bent = both_gelu(inner_sum)
                    value, bent = value.astype(jnp.bfloat16), bent.astype(jnp.bfloat16)
                    update = jnp.dot(
                        value,
                        held[k, pl.ds(3 * inner, inner), :],
                        preferred_element_type=jnp.float32,
                    )
                    results.append((value, bent, (old + update).astype(jnp.bfloat16)))
                for place, (value, bent, _) in zip(places, results):
                    active[k][pl.ds(place, tile), :] = value
                    bend[k][pl.ds(place, tile), :] = bent
                return [new for _, _, new in results]

            def spots(i, base):
                return [
                    pl.multiple_of(base + (i * team + g) * tile, 16) for g in range(team)
                ]

            if k < sections - 1:

                def step(i, carry, k=k):
                    places = spots(i, 0)
                    news = group(places)
                    pairs = [both_gelu(new.astype(jnp.float32)) for new in news]
                    for place, new, (value, bent) in zip(places, news, pairs):
                        state[pl.ds(place, tile), :] = new
                        ahead = pl.multiple_of(shifts[k + 1] + place, 16)
                        hidden[k + 1][pl.ds(ahead, tile), :] = value.astype(jnp.bfloat16)
                        slope[k][pl.ds(place, tile), :] = bent.astype(jnp.bfloat16)
                    return carry

                lax.fori_loop(0, length // (tile * team), step, 0)
                keep(hidden[k + 1].at[pl.ds(shifts[k + 1], length)], hidden_out[k + 1])
                keep(slope[k], slope_out[k])
            else:

                def finish_half(number):
                    def step(i, carry):
                        places = spots(i, number * half)
                        for place, new in zip(places, group(places)):
                            state[pl.ds(place, tile), :] = new
                        return carry

                    lax.fori_loop(0, steps // team, step, 0)

                finish_half(1 - c)
                theirs = state.at[pl.ds(pl.multiple_of((1 - c) * half, 16), half)]
                last = remote(theirs, top_ref.at[c], tsend, trecv, partner)
                last.start()
                finish_half(c)
                top_ref[c] = state[pl.ds(pl.multiple_of(c * half, 16), half), :]
            keep(active[k], active_out[k])
            keep(bend[k], bend_out[k])
        for copy in outs:
            copy.wait()
        last.wait()
        across.wait_send()
        for copy in first + second:
            copy.wait_send()

    bf16 = jnp.bfloat16
    long = jax.ShapeDtypeStruct((length, channels), bf16)
    thin = jax.ShapeDtypeStruct((length, inner), bf16)
    dma = pltpu.SemaphoreType.DMA
    copies = 4 * sections
    out = pl.pallas_call(
        kernel,
        out_shape=[
            jax.ShapeDtypeStruct((seqs, half, channels), bf16),
            jax.ShapeDtypeStruct((sections, rows, channels), bf16),
        ]
        + [long] * (2 * sections - 1)
        + [thin] * (2 * sections),
        in_specs=[ANY, pl.BlockSpec(memory_space=pltpu.VMEM), ANY, ANY],
        out_specs=[pl.BlockSpec(memory_space=pltpu.VMEM)] + [ANY] * (4 * sections),
        scratch_shapes=[
            pltpu.VMEM((seqs, half, width), jnp.int32),
            pltpu.VMEM((sections, rows, channels), bf16),
            pltpu.VMEM((3 * channels, inner), bf16),
            pltpu.VMEM((length, channels), bf16),
        ]
        + [pltpu.VMEM((length + 2 * by, channels), bf16) for by in shifts]
        + [pltpu.VMEM((length, channels), bf16)] * (sections - 1)
        + [pltpu.VMEM((length, inner), bf16)] * (2 * sections)
        + [dma, dma]
        + [dma((sections - 1,))] * 4
        + [dma, dma, dma((3,)), dma((copies,))],
        compiler_params=pltpu.CompilerParams(
            collective_id=0, has_side_effects=True, vmem_limit_bytes=54 * 2**20
        ),
        name="forward_tower",
    )(bases, stem, taps, proj)
    top, weights = out[:2]
    hidden, slope = out[2 : 2 + sections], out[2 + sections : 1 + 2 * sections]
    active = out[1 + 2 * sections : 1 + 3 * sections]
    bend = out[1 + 3 * sections :]
    return top, weights, hidden, slope, active, bend


def head(top, targets, head_weight, factor):
    seqs, half, channels = top.shape
    tracks = head_weight.shape[1]
    tile = tile_of(half)
    if half % 512 == 0:
        tile = 512
    steps = half // tile

    def kernel(
        top_ref, targets_ref, weight_ref, grad_ref, cot_ref, counts, stage, load, send, recv
    ):
        s, c = lax.axis_index("section"), lax.axis_index("seq")
        partner = {"section": s, "seq": 1 - c}
        loads = []
        for n, b in enumerate((1 - c, c)):
            for i in range(steps):
                loads.append(
                    pltpu.make_async_copy(
                        targets_ref.at[b, pl.ds(i * tile, tile)],
                        counts.at[n * steps + i],
                        load.at[n * steps + i],
                    )
                )
                loads[-1].start()
        greet([partner])
        grad_ref[...] = jnp.zeros_like(grad_ref)

        def run(b, n, store):
            def step(i, carry):
                at = pl.multiple_of(i * tile, 16)
                pltpu.make_async_copy(
                    targets_ref.at[b, pl.ds(at, tile)], counts.at[n + i], load.at[n + i]
                ).wait()
                value, bent = both_gelu(top_ref[b, pl.ds(at, tile), :].astype(jnp.float32))
                lifted = value.astype(jnp.bfloat16)
                logits = jnp.dot(lifted, weight_ref[...], preferred_element_type=jnp.float32)
                drop = jnp.exp(logits) - counts[n + i].astype(jnp.float32)
                drop = (drop * factor).astype(jnp.bfloat16)
                grad_ref[...] += contract_rows(lifted, drop)
                lift = times_transposed(drop, weight_ref[...])
                store(at, (lift * bent).astype(jnp.bfloat16))
                return carry

            lax.fori_loop(0, steps, step, 0)

        def away(at, value):
            stage[pl.ds(at, tile), :] = value

        def here(at, value):
            cot_ref[c, pl.ds(at, tile), :] = value

        run(1 - c, 0, away)
        copy = remote(stage, cot_ref.at[c], send, recv, partner)
        copy.start()
        run(c, steps, here)
        copy.wait()

    vmem = pl.BlockSpec(memory_space=pltpu.VMEM)
    dma = pltpu.SemaphoreType.DMA
    return pl.pallas_call(
        kernel,
        out_shape=[
            jax.ShapeDtypeStruct((channels, tracks), jnp.float32),
            jax.ShapeDtypeStruct(top.shape, jnp.bfloat16),
        ],
        in_specs=[vmem, ANY, vmem],
        out_specs=[vmem, vmem],
        scratch_shapes=[
            pltpu.VMEM((seqs * steps, tile, tracks), jnp.int32),
            pltpu.VMEM((half, channels), jnp.bfloat16),
            dma((seqs * steps,)),
            dma,
            dma,
        ],
        compiler_params=pltpu.CompilerParams(
            collective_id=1, has_side_effects=True, vmem_limit_bytes=48 * 2**20
        ),
        name="head",
    )(top, targets, head_weight)


def backward_tower(head_part, cot, weights, hidden, slope, active, bend, sections, zones, unit):
    length, channels = hidden[0].shape
    inner = active[0].shape[1]
    rows = weights.shape[1]
    part = rows // 2
    quarter = part // sections
    levels = zones.bit_length() - 1
    tracks = head_part.shape[1]
    side = head_part.shape[0] // 2
    tile = length // 2
    most = unit * 2 ** (sections - 1)
    f32, bf16 = jnp.float32, jnp.bfloat16

    def kernel(*refs):
        head_ref, cot_ref, weights_ref = refs[:3]
        refs = refs[3:]
        hidden_in, slope_in = refs[:sections], refs[sections : 2 * sections - 1]
        refs = refs[2 * sections - 1 :]
        active_in, bend_in = refs[:sections], refs[sections : 2 * sections]
        refs = refs[2 * sections :]
        out, head_out = refs[:2]
        hidden, slope, active, bend = refs[2:4], refs[4:6], refs[6:8], refs[8:10]
        held, grad, pull, sums, load = refs[10:15]
        met, wire, came, total, zcame, final = refs[15:21]
        hmet, hsum, hcame = refs[21:24]
        sems = refs[24:]

        s, c, d = (lax.axis_index(name) for name in ("section", "seq", "dp"))
        partner = {"section": s, "seq": 1 - c, "dp": d}
        order = [lax.rem(s + k, sections) for k in range(1, sections)]
        across = [{"section": o, "seq": c, "dp": d} for o in order]
        bits = [lax.rem(d // 2**t, 2) for t in range(levels)]
        along = [
            {"section": s, "seq": c, "dp": d + 2**t * (1 - 2 * bits[t])} for t in range(levels)
        ]
        count = [0]

        def fetch(src, dst):
            copy = pltpu.make_async_copy(src, dst, load.at[count[0]])
            count[0] += 1
            copy.start()
            return copy

        bring = {}

        def prefetch(k):
            slot = k % 2
            early = [
                fetch(weights_ref.at[k], held.at[k]),
                fetch(bend_in[k], bend[slot]),
                fetch(active_in[k], active[slot]),
            ]
            late = [fetch(hidden_in[k], hidden[slot])]
            if k:
                late.append(fetch(slope_in[k - 1], slope[slot]))
            bring[k] = (early, late)

        prefetch(sections - 1)
        greet([partner] + across + along)

        sends = []

        def launch(src, dst, pair, index, peer):
            copy = remote(src, dst, sems[2 * pair].at[index], sems[2 * pair + 1].at[index], peer)
            copy.start()
            sends.append(copy)
            return copy

        def block(base, size, number):
            return pl.ds(pl.multiple_of(base + number * size, 8), size)

        flight = {}

        def swap(k):
            far = sums.at[k, block(0, part, 1 - c)]
            flight[k] = [launch(far, met.at[k], 0, k, partner)]

        def spread(k):
            flight[k][0].wait_recv()
            flight[k] = []

            def both(o):
                return met[k, block(0, quarter, o), :] + sums[k, block(c * part, quarter, o), :]

            for n, o in enumerate(order):
                wire[k, n] = both(o).astype(bf16)
                flight[k].append(
                    launch(wire.at[k, n], came.at[k, n], 1, k * (sections - 1) + n, across[n])
                )
            total[k] = both(s)

        def kept(span, t):
            base = 0
            for step in range(t):
                base = base + bits[step] * (span >> (step + 1))
            return base

        def landing(span, t):
            return pl.ds(span - (span >> t), span >> (t + 1))

        def climb(k, t):
            for copy in flight[k]:
                copy.wait_recv()
            if t == 0:
                value = total[k]
                for n in range(sections - 1):
                    value = value + came[k, n].astype(f32)
                total[k] = value
            else:
                mine = block(kept(quarter, t), quarter >> t, 0)
                total[k, mine, :] = total[k, mine, :] + zcame[k, landing(quarter, t - 1), :]
            size = quarter >> (t + 1)
            away = block(kept(quarter, t), size, 1 - bits[t])
            flight[k] = [
                launch(
                    total.at[k, away],
                    zcame.at[k, landing(quarter, t)],
                    2,
                    k * levels + t,
                    along[t],
                )
            ]

        def level(k, t):
            for copy in flight[k]:
                copy.wait_recv()
            mine = block(kept(quarter, t + 1), quarter >> (t + 1), 0)
            if t == levels - 1:
                final[k, mine, :] = total[k, mine, :] + zcame[k, landing(quarter, t), :]
            piece = final.at[k, mine]
            flight[k] = [launch(piece, piece, 3, k * levels + t, along[t])]

        strip = quarter // zones
        floors = [lax.rem(d + n, zones) for n in range(1, zones)]
        lifts = [{"section": s, "seq": c, "dp": z} for z in floors]

        def climb_at_once():
            for copy in flight[0]:
                copy.wait_recv()
            value = total[0]
            for n in range(sections - 1):
                value = value + came[0, n].astype(f32)
            total[0] = value
            flight[0] = [
                launch(
                    total.at[0, block(0, strip, z)],
                    zcame.at[0, pl.ds(n * strip, strip)],
                    10,
                    n,
                    lifts[n],
                )
                for n, z in enumerate(floors)
            ]

        def level_at_once():
            for copy in flight[0]:
                copy.wait_recv()
            value = total[0, block(0, strip, d), :]
            for n in range(zones - 1):
                value = value + zcame[0, pl.ds(n * strip, strip), :]
            final[0, block(0, strip, d), :] = value
            piece = final.at[0, block(0, strip, d)]
            flight[0] = [launch(piece, piece, 11, n, peer) for n, peer in enumerate(lifts)]
            strip_home(d)

        def home_strip(z):
            owner = {"section": 0, "seq": c, "dp": d}
            index = lax.rem(s + sections - 1, sections) * zones + z
            place = out.at[block(c * part + s * quarter, strip, z)]
            return remote(
                final.at[0, block(0, strip, z)],
                place,
                sems[24].at[z],
                sems[25].at[index],
                owner,
            )

        def strip_home(z):
            @pl.when(s != 0)
            def _():
                home_strip(z).start()

        def deliver_strips():
            for n, copy in enumerate(flight[0]):
                copy.wait_recv()
                strip_home(lax.rem(d + zones - 1 - n, zones))

            @pl.when(s == 0)
            def _():
                out[block(c * part, quarter, s), :] = final[0]
                relay(0, s).start()

        def home(k):
            owner = {"section": k, "seq": c, "dp": d}
            index = lax.rem(s + 2 * sections - k - 1, sections)
            place = out.at[block(c * part, quarter, s)]
            return remote(final.at[k], place, sems[8].at[k], sems[9].at[index], owner)

        def deliver(k):
            for copy in flight[k]:
                copy.wait_recv()

            @pl.when(s != k)
            def _():
                home(k).start()

            @pl.when(s == k)
            def _():
                out[block(c * part, quarter, s), :] = final[k]
                relay(0, s).start()

        def relay(n, source):
            piece = out.at[block(c * part, quarter, source)]
            return remote(piece, piece, sems[10].at[n], sems[11].at[n], partner)

        def hand(k):
            @pl.when(s == k)
            def _():
                for n, o in enumerate(order):
                    if k:
                        piece = out.at[block(c * part, quarter, o)]
                        remote(
                            final.at[k], piece, sems[8].at[k], sems[9].at[n], across[n]
                        ).wait_recv()
                    else:
                        for z in range(zones):
                            piece = out.at[block(c * part + o * quarter, strip, z)]
                            remote(
                                final.at[0, block(0, strip, z)],
                                piece,
                                sems[24].at[z],
                                sems[25].at[n * zones + z],
                                across[n],
                            ).wait_recv()
                    relay(n + 1, o).start()

        def settle(k):
            @pl.when(s != k)
            def _():
                if k:
                    home(k).wait_send()
                else:
                    for z in range(zones):
                        home_strip(z).wait_send()

            @pl.when(s == k)
            def _():
                for n, o in enumerate([s] + order):
                    relay(n, o).wait()

        def head_swap():
            far = head_ref.at[block(0, side, 1 - c)]
            flight["h"] = [launch(far, hmet, 6, 0, partner)]

        def head_climb(t):
            flight["h"][0].wait_recv()
            if t == 0:
                hsum[...] = hmet[...] + head_ref[block(0, side, c), :]
            else:
                mine = block(kept(side, t), side >> t, 0)
                hsum[mine, :] = hsum[mine, :] + hcame[landing(side, t - 1), :]
            away = block(kept(side, t), side >> (t + 1), 1 - bits[t])
            flight["h"] = [
                launch(hsum.at[away], hcame.at[landing(side, t)], 7, t, along[t])
            ]

        flight["r"] = []

        def pass_on(start, size):
            piece = head_out.at[block(c * side + start, size, 0)]
            flight["r"].append(launch(piece, piece, 9, len(flight["r"]), partner))

        def other(span, t):
            return kept(span, t) + (1 - bits[t]) * (span >> (t + 1))

        def head_level(t):
            flight["h"][0].wait_recv()
            start, size = kept(side, t + 1), side >> (t + 1)
            place = block(c * side + start, size, 0)
            if t == levels - 1:
                mine = block(start, size, 0)
                head_out[place, :] = hsum[mine, :] + hcame[landing(side, t), :]
                pass_on(start, size)
            else:
                pass_on(other(side, t + 1), side >> (t + 2))
            piece = head_out.at[place]
            flight["h"] = [launch(piece, piece, 8, t, along[t])]

        def head_hand():
            flight["h"][0].wait_recv()
            pass_on(other(side, 0), side // 2)

        head_swap()
        pull[pl.ds(0, most), :] = jnp.zeros((most, inner), bf16)
        pull[pl.ds(most + length, most), :] = jnp.zeros((most, inner), bf16)
        sums[...] = jnp.zeros_like(sums)

        top = sections - 1
        stages = {}
        for k in range(sections):
            line = [lambda k=k: swap(k), lambda k=k: spread(k)]
            if k:
                line += [lambda k=k, t=t: climb(k, t) for t in range(levels)]
                line += [lambda k=k, t=t: level(k, t) for t in reversed(range(levels))]
                line.append(lambda k=k: deliver(k))
            else:
                line += [climb_at_once, level_at_once, deliver_strips]
            stages[k] = line + [lambda k=k: hand(k)]
        line = [lambda t=t: head_climb(t) for t in range(levels)]
        line += [lambda t=t: head_level(t) for t in reversed(range(levels))]
        stages["h"] = line + [head_hand]
        marks = {}

        def plan(name, ticks):
            for at in ticks:
                if at <= 3 * sections - 1 and stages[name]:
                    marks.setdefault(at, []).append(stages[name].pop(0))

        for k in range(sections):
            plan(k, [3 * (top - k) + 2 + gap for gap in (0, 2, 3, 6, 9)])
        plan("h", (1, 5, 10))
        clock = [0]

        def tick():
            for stage in marks.get(clock[0], []):
                stage()
            clock[0] += 1

        for k in reversed(range(sections)):
            by = unit * 2**k
            slot = k % 2
            above = cot_ref if k == top else grad
            if k:
                prefetch(k - 1)
            for copy in bring[k][0]:
                copy.wait()

            def inward(i, k=k, slot=slot, above=above):
                place = i * tile
                here = above[pl.ds(place, tile), :]
                back = times_transposed(here, held[k, pl.ds(3 * inner, inner), :])
                back = back * bend[slot][pl.ds(place, tile), :].astype(f32)
                pull[pl.ds(most + place, tile), :] = back.astype(bf16)
                sums[k, pl.ds(3 * inner, inner), :] += contract_rows(
                    active[slot][pl.ds(place, tile), :], here
                )

            for i in range(length // tile):
                inward(i)
                tick()
            for copy in bring[k][1]:
                copy.wait()

            def outward(i, carry, k=k, by=by, slot=slot, above=above):
                place = pl.multiple_of(i * tile, 16)
                there = hidden[slot][pl.ds(place, tile), :]
                value = None
                for j in range(3):
                    piece = pull[pl.ds(pl.multiple_of(most + place + (1 - j) * by, 16), tile), :]
                    span = pl.ds(j * inner, inner)
                    sums[k, span, :] += contract_rows(piece, there)
                    if k:
                        term = jnp.dot(piece, held[k, span, :], preferred_element_type=f32)
                        value = term if value is None else value + term
                if k:
                    value = value * slope[slot][pl.ds(place, tile), :].astype(f32)
                    value = value + above[pl.ds(place, tile), :].astype(f32)
                    grad[pl.ds(place, tile), :] = value.astype(bf16)
                return carry

            lax.fori_loop(0, length // tile, outward, 0)
            tick()

        rounds = 0
        while any(stages.values()):
            for name in [*reversed(range(2, sections)), 0, 1, "h"]:
                if stages[name] and (name != "h" or rounds > 1):
                    stages[name].pop(0)()
            rounds += 1
        for copy in flight["r"]:
            copy.wait_recv()
        for k in range(sections):
            settle(k)
        for copy in sends:
            copy.wait_send()

    dma = pltpu.SemaphoreType.DMA

    def pair(count):
        return [dma((count,))] * 2

    long, thin = pltpu.VMEM((length, channels), bf16), pltpu.VMEM((length, inner), bf16)
    vmem = pl.BlockSpec(memory_space=pltpu.VMEM)
    return pl.pallas_call(
        kernel,
        out_shape=[
            jax.ShapeDtypeStruct((rows, channels), f32),
            jax.ShapeDtypeStruct(head_part.shape, f32),
        ],
        in_specs=[vmem, vmem] + [ANY] * (4 * sections),
        out_specs=[vmem, vmem],
        scratch_shapes=[long] * 4
        + [thin] * 4
        + [
            pltpu.VMEM(weights.shape, bf16),
            long,
            pltpu.VMEM((length + 2 * most, inner), bf16),
            pltpu.VMEM((sections, rows, channels), f32),
            dma((5 * sections,)),
            pltpu.VMEM((sections, part, channels), f32),
            pltpu.VMEM((sections, sections - 1, quarter, channels), bf16),
            pltpu.VMEM((sections, sections - 1, quarter, channels), bf16),
            pltpu.VMEM((sections, quarter, channels), f32),
            pltpu.VMEM((sections, quarter, channels), f32),
            pltpu.VMEM((sections, quarter, channels), f32),
            pltpu.VMEM((side, tracks), f32),
            pltpu.VMEM((side, tracks), f32),
            pltpu.VMEM((side, tracks), f32),
        ]
        + pair(sections)
        + pair(sections * (sections - 1))
        + pair(sections * levels)
        + pair(sections * levels)
        + [dma((sections,)), dma((sections,))]
        + pair(sections)
        + pair(1)
        + pair(levels)
        + pair(levels)
        + pair(levels + 1)
        + pair(zones - 1)
        + pair(zones - 1)
        + [dma((zones,)), dma((sections * zones,))],
        compiler_params=pltpu.CompilerParams(
            collective_id=2, has_side_effects=True, vmem_limit_bytes=48 * 2**20
        ),
        name="backward_tower",
    )(head_part, cot, weights, *hidden, *slope, *active, *bend)


def finish(total, head_sum, split):
    def kernel(total_ref, head_ref, conv_out, proj_out, head_out, sems):
        copies = [
            pltpu.make_async_copy(total_ref.at[pl.ds(0, split)], conv_out, sems.at[0]),
            pltpu.make_async_copy(
                total_ref.at[pl.ds(split, total.shape[0] - split)], proj_out, sems.at[1]
            ),
            pltpu.make_async_copy(head_ref, head_out, sems.at[2]),
        ]
        for copy in copies:
            copy.start()
        for copy in copies:
            copy.wait()

    width = total.shape[1]
    return pl.pallas_call(
        kernel,
        out_shape=[
            jax.ShapeDtypeStruct((split, width), total.dtype),
            jax.ShapeDtypeStruct((total.shape[0] - split, width), total.dtype),
            jax.ShapeDtypeStruct(head_sum.shape, head_sum.dtype),
        ],
        in_specs=[pl.BlockSpec(memory_space=pltpu.VMEM)] * 2,
        out_specs=[ANY] * 3,
        scratch_shapes=[pltpu.SemaphoreType.DMA((3,))],
        compiler_params=pltpu.CompilerParams(vmem_limit_bytes=8 * 2**20),
        name="finish",
    )(total, head_sum)


def plain_body(bases, targets, stem_weight, conv_weight, proj_weight, head_weight):
    sections = lax.axis_size("section")
    seqs = lax.axis_size("seq")
    section_number = lax.axis_index("section")
    batches, row_count, bin_width = bases.shape
    channels = stem_weight.shape[1]
    length = row_count * seqs
    factor = 1.0 / math.sqrt(batches * lax.axis_size("dp") * length)
    unit = length // 2**sections
    local_q = row_count // unit
    blocks = length // unit
    columns = batches * unit // (seqs * sections)

    conv_all = lax.all_gather(conv_weight, "section", axis=0, tiled=True)
    proj_all = lax.all_gather(proj_weight, "section", axis=0, tiled=True)

    def to_chains(value):
        value = lax.all_to_all(value, "seq", split_axis=1, concat_axis=0, tiled=True)
        return value.reshape(blocks * columns, value.shape[-1])

    own = bases.reshape(batches, local_q, unit, bin_width).transpose(1, 0, 2, 3)
    own = own.reshape(local_q, seqs, sections, columns, bin_width)
    own = lax.dynamic_index_in_dim(own, section_number, 2, keepdims=False)
    picked = to_chains(own.astype(jnp.bfloat16))
    onehot = jnp.concatenate([(picked == c).astype(jnp.bfloat16) for c in range(4)], 1)
    stem = stem_weight.reshape(bin_width, 4, channels).transpose(1, 0, 2).reshape(-1, channels)
    state = jnp.dot(onehot, stem, preferred_element_type=jnp.float32).astype(jnp.bfloat16)

    saved = []
    for layer in range(sections):
        by = columns * 2**layer
        taps = conv_all[layer].reshape(-1, conv_all.shape[-1])
        hidden = gelu_value(state.astype(jnp.float32)).astype(jnp.bfloat16)
        wide = jnp.concatenate([shift_rows(hidden, by), hidden, shift_rows(hidden, -by)], 1)
        inner_sum = jnp.dot(wide, taps, preferred_element_type=jnp.float32)
        active = gelu_value(inner_sum).astype(jnp.bfloat16)
        update = jnp.dot(active, proj_all[layer], preferred_element_type=jnp.float32)
        saved.append((state, wide, inner_sum, active))
        state = (state.astype(jnp.float32) + update).astype(jnp.bfloat16)

    lifted = gelu_value(state.astype(jnp.float32)).astype(jnp.bfloat16)
    lifted = lifted.reshape(seqs, local_q, 1, columns, channels)
    lifted = lax.all_to_all(lifted, "seq", split_axis=0, concat_axis=2, tiled=True)
    lifted = lifted.reshape(local_q, seqs, 1, columns, channels)
    lifted = lax.all_gather(lifted, "section", axis=2, tiled=True)
    lifted = lifted.reshape(local_q, batches, unit, channels).transpose(1, 0, 2, 3)
    lifted = lifted.reshape(batches * row_count, channels)

    logits = jnp.dot(lifted, head_weight, preferred_element_type=jnp.float32)
    counts = targets.reshape(batches * row_count, targets.shape[2]).astype(jnp.float32)
    slope = ((jnp.exp(logits) - counts) * factor).astype(jnp.bfloat16)
    head_sum = lax.psum(contract_rows(lifted, slope), ("seq", "dp"))
    lift_part = times_transposed(slope, head_weight)

    lift_part = lift_part.reshape(batches, local_q, unit, channels).transpose(1, 0, 2, 3)
    lift_part = lift_part.reshape(local_q, seqs, sections, columns, channels)
    lift_part = lax.psum_scatter(lift_part, "section", scatter_dimension=2, tiled=True)
    lift_grad = to_chains(lift_part.reshape(local_q, seqs, columns, channels))


    grad = (lift_grad * gelu_slope(state.astype(jnp.float32))).astype(jnp.bfloat16)
    parts = []
    for layer in reversed(range(sections)):
        by = columns * 2**layer
        start_state, wide, inner_sum, active = saved[layer]
        kernel = conv_all[layer]
        proj_part = contract_rows(active, grad)
        active_grad = times_transposed(grad, proj_all[layer])
        inner_grad = (active_grad * gelu_slope(inner_sum)).astype(jnp.bfloat16)
        parts.append(jnp.concatenate([contract_rows(inner_grad, wide), proj_part], 1))
        wide_grad = jnp.concatenate(
            [shift_rows(inner_grad, -by), inner_grad, shift_rows(inner_grad, by)], 1
        )
        turned = kernel.transpose(0, 2, 1).reshape(-1, channels)
        hidden_grad = jnp.dot(wide_grad, turned, preferred_element_type=jnp.float32)
        grad = (
            grad.astype(jnp.float32) + hidden_grad * gelu_slope(start_state.astype(jnp.float32))
        ).astype(jnp.bfloat16)
    parts = jnp.stack(parts[::-1])
    total = lax.psum_scatter(parts, "section", scatter_dimension=0, tiled=True)
    total = lax.psum(total[0], ("seq", "dp"))
    taps_width = total.shape[1] - channels
    conv_sum = total[:, :taps_width].T.reshape(conv_weight.shape)
    return conv_sum, total[:, taps_width:][None], head_sum


def paired_body(bases, targets, stem_weight, conv_weight, proj_weight, head_weight):
    sections = lax.axis_size("section")
    zones = lax.axis_size("dp")
    batches, half, bin_width = bases.shape
    channels = stem_weight.shape[1]
    inner = proj_weight.shape[1]
    length = batches * half
    unit = length // 2**sections
    factor = 1.0 / math.sqrt(batches * zones * length)
    stem = stem_weight.reshape(bin_width, 4, channels).transpose(1, 0, 2).reshape(-1, channels)
    taps = conv_weight[0].transpose(0, 2, 1).reshape(3 * inner, channels)
    top, weights, hidden, slope, active, bend = forward_tower(
        bases, stem, taps, proj_weight[0], sections, unit
    )
    head_part, cot = head(top, targets, head_weight, factor)
    cot = cot.reshape(length, channels)
    total, head_sum = backward_tower(
        head_part, cot, weights, hidden, slope, active, bend, sections, zones, unit
    )
    conv_sum, proj_sum, head_sum = finish(total, head_sum, 3 * inner)
    conv_sum = conv_sum.reshape(3, inner, channels).transpose(0, 2, 1)
    return conv_sum[None], proj_sum[None], head_sum


def body(bases, targets, stem_weight, conv_weight, proj_weight, head_weight):
    sections, zones = lax.axis_size("section"), lax.axis_size("dp")
    batches, half = bases.shape[:2]
    inner = proj_weight.shape[1]
    unit = batches * half // 2**sections
    paired = lax.axis_size("seq") == 2 and batches == 2 and zones > 1 and sections > 1
    paired = paired and unit % 16 == 0 and half % 16 == 0 and inner % 16 == 0
    paired = paired and (2 * inner) % (16 * sections) == 0
    paired = paired and (2 * inner) % (8 * sections * zones) == 0
    paired = paired and zones & (zones - 1) == 0
    paired = paired and stem_weight.shape[1] % (16 * zones) == 0
    run = paired_body if paired else plain_body
    return run(bases, targets, stem_weight, conv_weight, proj_weight, head_weight)


def solution(mesh):
    in_specs = (
        P("dp", "seq", None),
        P("dp", "seq", "section"),
        P(),
        P("section", None, None, None),
        P("section", None, None),
        P(None, "section"),
    )
    out_specs = (P("section", None, None, None), P("section", None, None), P(None, "section"))
    return jax.shard_map(body, mesh=mesh, in_specs=in_specs, out_specs=out_specs, check_vma=False)
```

profile of v0, /device:TPU:0, one launch (start us, length us, event | category | flops | bytes accessed | tf_op | source)
XLA Modules:
  0.0 135.9 jit_solution(17895609357886918450)
XLA Ops:
  0.6 1.1 reshape.21
  1.7 0.0 copy-start.2
  1.7 0.8 copy.9
  2.5 46.2 %forward_tower.1 = (bf16[2,1536,384]{2,1,0:T(8,128)(2,1)}, bf16[4,768,384]{2,1,0:T(8,128)(2,1)}, bf16[3072,384]{1,0:T(8,128)(2,1)}, bf16[3072,384]{1,0:T(8,128)(...) custom-call(s32[2,1536,128]{2,1,0:T(8,128)} %refs_0_.1, ...), custom_call_target="tpu_custom_call" | custom-call | tf_op jit(solution)/shard_map/forward_tower/pallas_call | solution.py:270
  48.8 0.0 copy-done.2
  48.8 0.0 copy-start.1
  48.8 13.9 %head.1 = (f32[384,1024]{1,0:T(8,128)S(1)}, bf16[2,1536,384]{2,1,0:T(8,128)(2,1)S(1)}) custom-call(bf16[2,1536,384]{2,1,0:T(8,128)(2,1)} %get-tuple-element.27.top_ref, s32[2,1536,1024]{2,1,0:T(8,128)} %targets_ref.1, bf16[384,1024]{1,0:T(8,128)(2,1)S(1)} %copy-done.2), custom_call_target="tpu_custom_call" | custom-call | tf_op jit(solution)/shard_map/head/pallas_call | solution.py:363
  62.7 0.0 copy-start
  62.7 1.4 %copy-done = bf16[2,1536,384]{2,1,0:T(8,128)(2,1)} copy-done((bf16[2,1536,384]{2,1,0:T(8,128)(2,1)}, bf16[2,1536,384]{2,1,0:T(8,128)(2,1)S(1)}, u32[]{:S(2)}) %copy-start) | copy-done | bytes 2359320
  64.0 0.0 copy-done.1
  64.0 70.1 %backward_tower.1 = (f32[768,384]{1,0:T(8,128)S(1)}, f32[384,1024]{1,0:T(8,128)S(1)}) custom-call(f32[384,1024]{1,0:T(8,128)S(1)} %get-tuple-element.28.refs_0_, bf16[3072,384]{1,0:T(8,128)(2,1)} %bitcast.16, bf16[4,768,384]{2,1,0:T(8,128)(2,1)} %get-tuple-element.30.refs_2_, bf16[3072,384]{1,0:T(8,128)(2,1)} %get-tuple-element.31.refs_3_, ...), custom_call_target="tpu_custom_call" | custom-call | tf_op jit(solution)/shard_map/backward_tower/pallas_call | solution.py:778
  134.1 1.6 %finish.1 = (f32[576,384]{1,0:T(8,128)}, f32[192,384]{1,0:T(8,128)}, f32[384,1024]{1,0:T(8,128)}) custom-call(f32[768,384]{1,0:T(8,128)S(1)} %get-tuple-element.46.total_ref, f32[384,1024]{1,0:T(8,128)S(1)} %get-tuple-element.47.head_ref), custom_call_target="tpu_custom_call" | custom-call | tf_op jit(solution)/shard_map/finish/pallas_call | solution.py:839
Async XLA Ops:
  1.7 47.0 %copy-start.2 = (bf16[384,1024]{1,0:T(8,128)(2,1)S(1)}, bf16[384,1024]{1,0:T(8,128)(2,1)}, u32[]{:S(2)}) copy-start(bf16[384,1024]{1,0:T(8,128)(2,1)} %weight_ref.1) | copy-start | bytes 2359300
  48.8 15.3 %copy-start.1 = (bf16[3072,192]{1,0:T(8,128)(2,1)S(1)}, bf16[3072,192]{1,0:T(8,128)(2,1)}, u32[]{:S(2)}) copy-start(bf16[3072,192]{1,0:T(8,128)(2,1)} %get-tuple-element.38.refs_10_) | copy-start | bytes 3538948
  62.7 1.4 %copy-start = (bf16[2,1536,384]{2,1,0:T(8,128)(2,1)}, bf16[2,1536,384]{2,1,0:T(8,128)(2,1)S(1)}, u32[]{:S(2)}) copy-start(bf16[2,1536,384]{2,1,0:T(8,128)(2,1)S(1)} %get-tuple-element.29) | copy-start | bytes 7077892
where the time goes:
time: 136 us
  Pallas kernels  132 us (97%)
  local copies, waits for them, and re-layouts  3.27 us (2%)
    pallas_call x1, Pallas kernels, backward_tower(): pl.pallas_call(kernel, out_shape=[jax.ShapeDtypeStruct((rows, channels),...  70.1 us
    pallas_call x1, Pallas kernels, forward_tower(): pl.pallas_call(kernel, out_shape=[jax.ShapeDtypeStruct((seqs, half, chann...  46.2 us
    pallas_call x1, Pallas kernels, head(): pl.pallas_call(kernel, out_shape=[jax.ShapeDtypeStruct((channels, tracks)...  13.9 us

commit v1 on v0

--- a/solution.py
+++ b/solution.py
@@ -102,8 +102,8 @@
         refs = refs[1 + 2 * sections :]
         active_out, bend_out = refs[:sections], refs[sections : 2 * sections]
         refs = refs[2 * sections :]
-        full, held, turned, state = refs[:4]
-        refs = refs[4:]
+        full, held, turned, state, sorted_stem = refs[:5]
+        refs = refs[5:]
         hidden, slope = refs[:sections], refs[sections : 2 * sections - 1]
         refs = refs[2 * sections - 1 :]
         active, bend = refs[:sections], refs[sections : 2 * sections]
@@ -134,10 +134,18 @@
         for k, peer in enumerate(peers):
             first.append(remote(mine, mine, send.at[k], recv.at[k], peer))
             first[-1].start()
-        for k in range(sections):
+        for k in range(sections - 1):
             edge = jnp.zeros((shifts[k], channels), jnp.bfloat16)
             hidden[k][pl.ds(0, shifts[k]), :] = edge
             hidden[k][pl.ds(shifts[k] + length, shifts[k]), :] = edge
+
+        across_rows = lax.broadcasted_iota(jnp.int32, (4 * width, 4 * width), 0)
+        across_columns = lax.broadcasted_iota(jnp.int32, (4 * width, 4 * width), 1)
+        place_of = 4 * lax.rem(across_rows, width) + across_rows // width
+        chosen = (across_columns == place_of).astype(jnp.bfloat16)
+        sorted_stem[...] = jnp.dot(
+            chosen, stem_ref[...], preferred_element_type=jnp.float32
+        ).astype(jnp.bfloat16)
 
         def begin(number):
             def step(i, carry):
@@ -146,7 +154,7 @@
                 onehot = jnp.concatenate(
                     [(codes == k).astype(jnp.bfloat16) for k in range(4)], 1
                 )
-                start = jnp.dot(onehot, stem_ref[...], preferred_element_type=jnp.float32)
+                start = jnp.dot(onehot, sorted_stem[...], preferred_element_type=jnp.float32)
                 start = start.astype(jnp.bfloat16)
                 place = pl.multiple_of(number * half + at, 16)
                 state[pl.ds(place, tile), :] = start
@@ -186,18 +194,19 @@
                 tap = held[k, pl.ds(j * inner, inner), :]
                 turned[pl.ds(j * channels, channels), :] = tap.T
 
-            def group(places, k=k, by=by):
+            def group(places, lead, width, k=k, by=by):
+                weight = turned[pl.ds(pl.multiple_of(lead * channels, 16), width * channels), :]
                 inners = []
                 for place in places:
                     wide = jnp.concatenate(
                         [
-                            hidden[k][pl.ds(pl.multiple_of(place + j * by, 16), tile), :]
-                            for j in range(3)
+                            hidden[k][pl.ds(pl.multiple_of(place + (lead + j) * by, 16), tile), :]
+                            for j in range(width)
                         ],
                         1,
                     )
                     inners.append(
-                        jnp.dot(wide, turned[...], preferred_element_type=jnp.float32)
+                        jnp.dot(wide, weight, preferred_element_type=jnp.float32)
                     )
                 olds = [state[pl.ds(place, tile), :].astype(jnp.float32) for place in places]
                 results = []
@@ -224,7 +233,7 @@
 
                 def step(i, carry, k=k):
                     places = spots(i, 0)
-                    news = group(places)
+                    news = group(places, 0, 3)
                     pairs = [both_gelu(new.astype(jnp.float32)) for new in news]
                     for place, new, (value, bent) in zip(places, news, pairs):
                         state[pl.ds(place, tile), :] = new
@@ -241,7 +250,7 @@
                 def finish_half(number):
                     def step(i, carry):
                         places = spots(i, number * half)
-                        for place, new in zip(places, group(places)):
+                        for place, new in zip(places, group(places, 1 - number, 2)):
                             state[pl.ds(place, tile), :] = new
                         return carry
 
@@ -282,6 +291,7 @@
             pltpu.VMEM((sections, rows, channels), bf16),
             pltpu.VMEM((3 * channels, inner), bf16),
             pltpu.VMEM((length, channels), bf16),
+            pltpu.VMEM(stem.shape, bf16),
         ]
         + [pltpu.VMEM((length + 2 * by, channels), bf16) for by in shifts]
         + [pltpu.VMEM((length, channels), bf16)] * (sections - 1)
@@ -417,6 +427,8 @@
         along = [
             {"section": s, "seq": c, "dp": d + 2**t * (1 - 2 * bits[t])} for t in range(levels)
         ]
+        floors = [lax.rem(d + n, zones) for n in range(1, zones)]
+        lifts = [{"section": s, "seq": c, "dp": z} for z in floors]
         count = [0]
 
         def fetch(src, dst):
@@ -440,7 +452,7 @@
             bring[k] = (early, late)
 
         prefetch(sections - 1)
-        greet([partner] + across + along)
+        greet([partner] + across + lifts)
 
         sends = []
 
@@ -515,8 +527,6 @@
             flight[k] = [launch(piece, piece, 3, k * levels + t, along[t])]
 
         strip = quarter // zones
-        floors = [lax.rem(d + n, zones) for n in range(1, zones)]
-        lifts = [{"section": s, "seq": c, "dp": z} for z in floors]
 
         def climb_at_once():
             for copy in flight[0]:
@@ -636,43 +646,35 @@
             far = head_ref.at[block(0, side, 1 - c)]
             flight["h"] = [launch(far, hmet, 6, 0, partner)]
 
-        def head_climb(t):
+        band = side // zones
+
+        def head_climb():
             flight["h"][0].wait_recv()
-            if t == 0:
-                hsum[...] = hmet[...] + head_ref[block(0, side, c), :]
-            else:
-                mine = block(kept(side, t), side >> t, 0)
-                hsum[mine, :] = hsum[mine, :] + hcame[landing(side, t - 1), :]
-            away = block(kept(side, t), side >> (t + 1), 1 - bits[t])
+            hsum[...] = hmet[...] + head_ref[block(0, side, c), :]
             flight["h"] = [
-                launch(hsum.at[away], hcame.at[landing(side, t)], 7, t, along[t])
+                launch(
+                    hsum.at[block(0, band, z)], hcame.at[pl.ds(n * band, band)], 7, n, lifts[n]
+                )
+                for n, z in enumerate(floors)
             ]
 
-        flight["r"] = []
-
-        def pass_on(start, size):
-            piece = head_out.at[block(c * side + start, size, 0)]
-            flight["r"].append(launch(piece, piece, 9, len(flight["r"]), partner))
-
-        def other(span, t):
-            return kept(span, t) + (1 - bits[t]) * (span >> (t + 1))
-
-        def head_level(t):
-            flight["h"][0].wait_recv()
-            start, size = kept(side, t + 1), side >> (t + 1)
-            place = block(c * side + start, size, 0)
-            if t == levels - 1:
-                mine = block(start, size, 0)
-                head_out[place, :] = hsum[mine, :] + hcame[landing(side, t), :]
-                pass_on(start, size)
-            else:
-                pass_on(other(side, t + 1), side >> (t + 2))
-            piece = head_out.at[place]
-            flight["h"] = [launch(piece, piece, 8, t, along[t])]
+        def head_level():
+            for copy in flight["h"]:
+                copy.wait_recv()
+            value = hsum[block(0, band, d), :]
+            for n in range(zones - 1):
+                value = value + hcame[pl.ds(n * band, band), :]
+            head_out[block(c * side, band, d), :] = value
+            mine = head_out.at[block(c * side, band, d)]
+            flight["h"] = [launch(mine, mine, 8, n, peer) for n, peer in enumerate(lifts)]
+            flight["r"] = [launch(mine, mine, 9, 0, partner)]
 
         def head_hand():
-            flight["h"][0].wait_recv()
-            pass_on(other(side, 0), side // 2)
+            for n, copy in enumerate(flight["h"]):
+                copy.wait_recv()
+                source = lax.rem(d + zones - 1 - n, zones)
+                piece = head_out.at[block(c * side, band, source)]
+                flight["r"].append(launch(piece, piece, 9, n + 1, partner))
 
         head_swap()
         pull[pl.ds(0, most), :] = jnp.zeros((most, inner), bf16)
@@ -690,9 +692,7 @@
             else:
                 line += [climb_at_once, level_at_once, deliver_strips]
             stages[k] = line + [lambda k=k: hand(k)]
-        line = [lambda t=t: head_climb(t) for t in range(levels)]
-        line += [lambda t=t: head_level(t) for t in reversed(range(levels))]
-        stages["h"] = line + [head_hand]
+        stages["h"] = [head_climb, head_level, head_hand]
         marks = {}
 
         def plan(name, ticks):
@@ -702,7 +702,7 @@
 
         for k in range(sections):
             plan(k, [3 * (top - k) + 2 + gap for gap in (0, 2, 3, 6, 9)])
-        plan("h", (1, 5, 10))
+        plan("h", (1, 8))
         clock = [0]
 
         def tick():
@@ -739,9 +739,14 @@
                 place = pl.multiple_of(i * tile, 16)
                 there = hidden[slot][pl.ds(place, tile), :]
                 value = None
-                for j in range(3):
-                    piece = pull[pl.ds(pl.multiple_of(most + place + (1 - j) * by, 16), tile), :]
-                    span = pl.ds(j * inner, inner)
+                for j in range(3 if k < top else 2):
+                    if k < top:
+                        start = pl.multiple_of(most + place + (1 - j) * by, 16)
+                        span = pl.ds(j * inner, inner)
+                    else:
+                        start = most + (1 - j) * by
+                        span = pl.ds(pl.multiple_of((i + j) * inner, 16), inner)
+                    piece = pull[pl.ds(start, tile), :]
                     sums[k, span, :] += contract_rows(piece, there)
                     if k:
                         term = jnp.dot(piece, held[k, span, :], preferred_element_type=f32)
@@ -808,9 +813,9 @@
         + [dma((sections,)), dma((sections,))]
         + pair(sections)
         + pair(1)
-        + pair(levels)
-        + pair(levels)
-        + pair(levels + 1)
+        + pair(zones - 1)
+        + pair(zones - 1)
+        + pair(zones)
         + pair(zones - 1)
         + pair(zones - 1)
         + [dma((zones,)), dma((sections * zones,))],
@@ -946,10 +951,9 @@
     length = batches * half
     unit = length // 2**sections
     factor = 1.0 / math.sqrt(batches * zones * length)
-    stem = stem_weight.reshape(bin_width, 4, channels).transpose(1, 0, 2).reshape(-1, channels)
     taps = conv_weight[0].transpose(0, 2, 1).reshape(3 * inner, channels)
     top, weights, hidden, slope, active, bend = forward_tower(
-        bases, stem, taps, proj_weight[0], sections, unit
+        bases, stem_weight, taps, proj_weight[0], sections, unit
     )
     head_part, cot = head(top, targets, head_weight, factor)
     cot = cot.reshape(length, channels)

time: 136 us -> 138 us (1.015)
  Pallas kernels: 132 us -> 135 us
  local copies, waits for them, and re-layouts: 3.27 us -> 1.38 us
    pallas_call x1, Pallas kernels: 70.1 us -> 74 us  [backward_tower(): pl.pallas_call(kernel, out_shape=[jax.ShapeDtypeStruct((rows, channels),...]
    reshape x2 -> x0, local copies, waits for them, and re-layouts: 1.88 us -> none  [paired_body(): stem_weight.reshape(bin_width, 4, channels).transpose(1, 0, 2)]
where the time goes in v1:
time: 138 us; the launch traced here: 137 us
  Pallas kernels  135 us (98%)
    pallas_call x1, Pallas kernels, backward_tower(): pl.pallas_call(kernel, out_shape=[jax.ShapeDtypeStruct((rows, channels),...  74 us
    pallas_call x1, Pallas kernels, forward_tower(): pl.pallas_call(kernel, out_shape=[jax.ShapeDtypeStruct((seqs, half, chann...  45.8 us
    pallas_call x1, Pallas kernels, head(): pl.pallas_call(kernel, out_shape=[jax.ShapeDtypeStruct((channels, tracks)...  13.9 us

profile of v1, /device:TPU:0, one launch (start us, length us, event | category | flops | bytes accessed | tf_op | source)
XLA Modules:
  0.0 137.5 jit_solution(6933354452927931386)
XLA Ops:
  0.6 0.0 copy-start.2
  0.6 45.8 %forward_tower.1 = (bf16[2,1536,384]{2,1,0:T(8,128)(2,1)}, bf16[4,768,384]{2,1,0:T(8,128)(2,1)}, bf16[3072,384]{1,0:T(8,128)(2,1)}, bf16[3072,384]{1,0:T(8,128)(...) custom-call(s32[2,1536,128]{2,1,0:T(8,128)} %refs_0_.1, ...), custom_call_target="tpu_custom_call" | custom-call | tf_op jit(solution)/shard_map/forward_tower/pallas_call | solution.py:279
  46.5 0.0 copy-done.2
  46.5 0.0 copy-start.1
  46.5 13.9 %head.1 = (f32[384,1024]{1,0:T(8,128)S(1)}, bf16[2,1536,384]{2,1,0:T(8,128)(2,1)S(1)}) custom-call(bf16[2,1536,384]{2,1,0:T(8,128)(2,1)} %get-tuple-element.27.top_ref, s32[2,1536,1024]{2,1,0:T(8,128)} %targets_ref.1, bf16[384,1024]{1,0:T(8,128)(2,1)S(1)} %copy-done.2), custom_call_target="tpu_custom_call" | custom-call | tf_op jit(solution)/shard_map/head/pallas_call | solution.py:373
  60.4 0.0 copy-start
  60.4 1.4 copy-done
  61.8 0.0 copy-done.1
  61.8 74.0 %backward_tower.1 = (f32[768,384]{1,0:T(8,128)S(1)}, f32[384,1024]{1,0:T(8,128)S(1)}) custom-call(f32[384,1024]{1,0:T(8,128)S(1)} %get-tuple-element.28.refs_0_, bf16[3072,384]{1,0:T(8,128)(2,1)} %bitcast.13, bf16[4,768,384]{2,1,0:T(8,128)(2,1)} %get-tuple-element.30.refs_2_, bf16[3072,384]{1,0:T(8,128)(2,1)} %get-tuple-element.31.refs_3_, ...), custom_call_target="tpu_custom_call" | custom-call | tf_op jit(solution)/shard_map/backward_tower/pallas_call | solution.py:783
  135.7 1.6 %finish.1 = (f32[576,384]{1,0:T(8,128)}, f32[192,384]{1,0:T(8,128)}, f32[384,1024]{1,0:T(8,128)}) custom-call(f32[768,384]{1,0:T(8,128)S(1)} %get-tuple-element.46.total_ref, f32[384,1024]{1,0:T(8,128)S(1)} %get-tuple-element.47.head_ref), custom_call_target="tpu_custom_call" | custom-call | tf_op jit(solution)/shard_map/finish/pallas_call | solution.py:844
Async XLA Ops:
  0.6 45.8 %copy-start.2 = (bf16[384,1024]{1,0:T(8,128)(2,1)S(1)}, bf16[384,1024]{1,0:T(8,128)(2,1)}, u32[]{:S(2)}) copy-start(bf16[384,1024]{1,0:T(8,128)(2,1)} %weight_ref.1) | copy-start | bytes 2359300
  46.5 15.3 %copy-start.1 = (bf16[3072,192]{1,0:T(8,128)(2,1)S(1)}, bf16[3072,192]{1,0:T(8,128)(2,1)}, u32[]{:S(2)}) copy-start(bf16[3072,192]{1,0:T(8,128)(2,1)} %get-tuple-element.38.refs_10_) | copy-start | bytes 3538948
  60.4 1.4 %copy-start = (bf16[2,1536,384]{2,1,0:T(8,128)(2,1)}, bf16[2,1536,384]{2,1,0:T(8,128)(2,1)S(1)}, u32[]{:S(2)}) copy-start(bf16[2,1536,384]{2,1,0:T(8,128)(2,1)S(1)} %get-tuple-element.29) | copy-start | bytes 7077892

commit v2 on v0

--- a/solution.py
+++ b/solution.py
@@ -102,8 +102,8 @@
         refs = refs[1 + 2 * sections :]
         active_out, bend_out = refs[:sections], refs[sections : 2 * sections]
         refs = refs[2 * sections :]
-        full, held, turned, state = refs[:4]
-        refs = refs[4:]
+        full, held, turned, state, sorted_stem = refs[:5]
+        refs = refs[5:]
         hidden, slope = refs[:sections], refs[sections : 2 * sections - 1]
         refs = refs[2 * sections - 1 :]
         active, bend = refs[:sections], refs[sections : 2 * sections]
@@ -134,10 +134,18 @@
         for k, peer in enumerate(peers):
             first.append(remote(mine, mine, send.at[k], recv.at[k], peer))
             first[-1].start()
-        for k in range(sections):
+        for k in range(sections - 1):
             edge = jnp.zeros((shifts[k], channels), jnp.bfloat16)
             hidden[k][pl.ds(0, shifts[k]), :] = edge
             hidden[k][pl.ds(shifts[k] + length, shifts[k]), :] = edge
+
+        across_rows = lax.broadcasted_iota(jnp.int32, (4 * width, 4 * width), 0)
+        across_columns = lax.broadcasted_iota(jnp.int32, (4 * width, 4 * width), 1)
+        place_of = 4 * lax.rem(across_rows, width) + across_rows // width
+        chosen = (across_columns == place_of).astype(jnp.bfloat16)
+        sorted_stem[...] = jnp.dot(
+            chosen, stem_ref[...], preferred_element_type=jnp.float32
+        ).astype(jnp.bfloat16)
 
         def begin(number):
             def step(i, carry):
@@ -146,7 +154,7 @@
                 onehot = jnp.concatenate(
                     [(codes == k).astype(jnp.bfloat16) for k in range(4)], 1
                 )
-                start = jnp.dot(onehot, stem_ref[...], preferred_element_type=jnp.float32)
+                start = jnp.dot(onehot, sorted_stem[...], preferred_element_type=jnp.float32)
                 start = start.astype(jnp.bfloat16)
                 place = pl.multiple_of(number * half + at, 16)
                 state[pl.ds(place, tile), :] = start
@@ -186,18 +194,19 @@
                 tap = held[k, pl.ds(j * inner, inner), :]
                 turned[pl.ds(j * channels, channels), :] = tap.T
 
-            def group(places, k=k, by=by):
+            def group(places, lead, width, k=k, by=by):
+                weight = turned[pl.ds(pl.multiple_of(lead * channels, 16), width * channels), :]
                 inners = []
                 for place in places:
                     wide = jnp.concatenate(
                         [
-                            hidden[k][pl.ds(pl.multiple_of(place + j * by, 16), tile), :]
-                            for j in range(3)
+                            hidden[k][pl.ds(pl.multiple_of(place + (lead + j) * by, 16), tile), :]
+                            for j in range(width)
                         ],
                         1,
                     )
                     inners.append(
-                        jnp.dot(wide, turned[...], preferred_element_type=jnp.float32)
+                        jnp.dot(wide, weight, preferred_element_type=jnp.float32)
                     )
                 olds = [state[pl.ds(place, tile), :].astype(jnp.float32) for place in places]
                 results = []
@@ -224,7 +233,7 @@
 
                 def step(i, carry, k=k):
                     places = spots(i, 0)
-                    news = group(places)
+                    news = group(places, 0, 3)
                     pairs = [both_gelu(new.astype(jnp.float32)) for new in news]
                     for place, new, (value, bent) in zip(places, news, pairs):
                         state[pl.ds(place, tile), :] = new
@@ -241,7 +250,7 @@
                 def finish_half(number):
                     def step(i, carry):
                         places = spots(i, number * half)
-                        for place, new in zip(places, group(places)):
+                        for place, new in zip(places, group(places, 1 - number, 2)):
                             state[pl.ds(place, tile), :] = new
                         return carry
 
@@ -282,6 +291,7 @@
             pltpu.VMEM((sections, rows, channels), bf16),
             pltpu.VMEM((3 * channels, inner), bf16),
             pltpu.VMEM((length, channels), bf16),
+            pltpu.VMEM(stem.shape, bf16),
         ]
         + [pltpu.VMEM((length + 2 * by, channels), bf16) for by in shifts]
         + [pltpu.VMEM((length, channels), bf16)] * (sections - 1)
@@ -417,6 +427,8 @@
         along = [
             {"section": s, "seq": c, "dp": d + 2**t * (1 - 2 * bits[t])} for t in range(levels)
         ]
+        floors = [lax.rem(d + n, zones) for n in range(1, zones)]
+        lifts = [{"section": s, "seq": c, "dp": z} for z in floors]
         count = [0]
 
         def fetch(src, dst):
@@ -440,7 +452,7 @@
             bring[k] = (early, late)
 
         prefetch(sections - 1)
-        greet([partner] + across + along)
+        greet([partner] + across + lifts)
 
         sends = []
 
@@ -515,63 +527,62 @@
             flight[k] = [launch(piece, piece, 3, k * levels + t, along[t])]
 
         strip = quarter // zones
-        floors = [lax.rem(d + n, zones) for n in range(1, zones)]
-        lifts = [{"section": s, "seq": c, "dp": z} for z in floors]
-
-        def climb_at_once():
-            for copy in flight[0]:
+        brisk = 0
+
+        def climb_at_once(k):
+            for copy in flight[k]:
                 copy.wait_recv()
-            value = total[0]
+            value = total[k]
             for n in range(sections - 1):
-                value = value + came[0, n].astype(f32)
-            total[0] = value
-            flight[0] = [
+                value = value + came[k, n].astype(f32)
+            total[k] = value
+            flight[k] = [
                 launch(
-                    total.at[0, block(0, strip, z)],
-                    zcame.at[0, pl.ds(n * strip, strip)],
+                    total.at[k, block(0, strip, z)],
+                    zcame.at[k, pl.ds(n * strip, strip)],
                     10,
-                    n,
+                    k * (zones - 1) + n,
                     lifts[n],
                 )
                 for n, z in enumerate(floors)
             ]
 
-        def level_at_once():
-            for copy in flight[0]:
+        def level_at_once(k):
+            for copy in flight[k]:
                 copy.wait_recv()
-            value = total[0, block(0, strip, d), :]
+            value = total[k, block(0, strip, d), :]
             for n in range(zones - 1):
-                value = value + zcame[0, pl.ds(n * strip, strip), :]
-            final[0, block(0, strip, d), :] = value
-            piece = final.at[0, block(0, strip, d)]
-            flight[0] = [launch(piece, piece, 11, n, peer) for n, peer in enumerate(lifts)]
-            strip_home(d)
-
-        def home_strip(z):
-            owner = {"section": 0, "seq": c, "dp": d}
-            index = lax.rem(s + sections - 1, sections) * zones + z
+                value = value + zcame[k, pl.ds(n * strip, strip), :]
+            final[k, block(0, strip, d), :] = value
+            piece = final.at[k, block(0, strip, d)]
+            flight[k] = [launch(piece, piece, 11, k * (zones - 1) + n, peer) for n, peer in enumerate(lifts)]
+            strip_home(k, d)
+
+        def home_strip(k, z):
+            owner = {"section": k, "seq": c, "dp": d}
+            index = lax.rem(s + 2 * sections - k - 1, sections) * zones + z
             place = out.at[block(c * part + s * quarter, strip, z)]
             return remote(
-                final.at[0, block(0, strip, z)],
+                final.at[k, block(0, strip, z)],
                 place,
-                sems[24].at[z],
+                sems[24].at[k * zones + z],
                 sems[25].at[index],
                 owner,
             )
 
-        def strip_home(z):
-            @pl.when(s != 0)
+        def strip_home(k, z):
+            @pl.when(s != k)
             def _():
-                home_strip(z).start()
-
-        def deliver_strips():
-            for n, copy in enumerate(flight[0]):
+                home_strip(k, z).start()
+
+        def deliver_strips(k):
+            for n, copy in enumerate(flight[k]):
                 copy.wait_recv()
-                strip_home(lax.rem(d + zones - 1 - n, zones))
-
-            @pl.when(s == 0)
+                strip_home(k, lax.rem(d + zones - 1 - n, zones))
+
+            @pl.when(s == k)
             def _():
-                out[block(c * part, quarter, s), :] = final[0]
+                out[block(c * part, quarter, s), :] = final[k]
                 relay(0, s).start()
 
         def home(k):
@@ -601,7 +612,7 @@
             @pl.when(s == k)
             def _():
                 for n, o in enumerate(order):
-                    if k:
+                    if k > brisk:
                         piece = out.at[block(c * part, quarter, o)]
                         remote(
                             final.at[k], piece, sems[8].at[k], sems[9].at[n], across[n]
@@ -610,9 +621,9 @@
                         for z in range(zones):
                             piece = out.at[block(c * part + o * quarter, strip, z)]
                             remote(
-                                final.at[0, block(0, strip, z)],
+                                final.at[k, block(0, strip, z)],
                                 piece,
-                                sems[24].at[z],
+                                sems[24].at[k * zones + z],
                                 sems[25].at[n * zones + z],
                                 across[n],
                             ).wait_recv()
@@ -621,11 +632,11 @@
         def settle(k):
             @pl.when(s != k)
             def _():
-                if k:
+                if k > brisk:
                     home(k).wait_send()
                 else:
                     for z in range(zones):
-                        home_strip(z).wait_send()
+                        home_strip(k, z).wait_send()
 
             @pl.when(s == k)
             def _():
@@ -683,12 +694,13 @@
         stages = {}
         for k in range(sections):
             line = [lambda k=k: swap(k), lambda k=k: spread(k)]
-            if k:
+            if k > brisk:
                 line += [lambda k=k, t=t: climb(k, t) for t in range(levels)]
                 line += [lambda k=k, t=t: level(k, t) for t in reversed(range(levels))]
                 line.append(lambda k=k: deliver(k))
             else:
-                line += [climb_at_once, level_at_once, deliver_strips]
+                for stage in (climb_at_once, level_at_once, deliver_strips):
+                    line.append(lambda k=k, stage=stage: stage(k))
             stages[k] = line + [lambda k=k: hand(k)]
         line = [lambda t=t: head_climb(t) for t in range(levels)]
         line += [lambda t=t: head_level(t) for t in reversed(range(levels))]
@@ -739,9 +751,14 @@
                 place = pl.multiple_of(i * tile, 16)
                 there = hidden[slot][pl.ds(place, tile), :]
                 value = None
-                for j in range(3):
-                    piece = pull[pl.ds(pl.multiple_of(most + place + (1 - j) * by, 16), tile), :]
-                    span = pl.ds(j * inner, inner)
+                for j in range(3 if k < top else 2):
+                    if k < top:
+                        start = pl.multiple_of(most + place + (1 - j) * by, 16)
+                        span = pl.ds(j * inner, inner)
+                    else:
+                        start = most + (1 - j) * by
+                        span = pl.ds(pl.multiple_of((i + j) * inner, 16), inner)
+                    piece = pull[pl.ds(start, tile), :]
                     sums[k, span, :] += contract_rows(piece, there)
                     if k:
                         term = jnp.dot(piece, held[k, span, :], preferred_element_type=f32)
@@ -757,7 +774,7 @@
 
         rounds = 0
         while any(stages.values()):
-            for name in [*reversed(range(2, sections)), 0, 1, "h"]:
+            for name in [0, *reversed(range(1, sections)), "h"]:
                 if stages[name] and (name != "h" or rounds > 1):
                     stages[name].pop(0)()
             rounds += 1
@@ -811,9 +828,9 @@
         + pair(levels)
         + pair(levels)
         + pair(levels + 1)
-        + pair(zones - 1)
-        + pair(zones - 1)
-        + [dma((zones,)), dma((sections * zones,))],
+        + pair(sections * (zones - 1))
+        + pair(sections * (zones - 1))
+        + [dma((sections * zones,)), dma((sections * zones,))],
         compiler_params=pltpu.CompilerParams(
             collective_id=2, has_side_effects=True, vmem_limit_bytes=48 * 2**20
         ),
@@ -946,10 +963,9 @@
     length = batches * half
     unit = length // 2**sections
     factor = 1.0 / math.sqrt(batches * zones * length)
-    stem = stem_weight.reshape(bin_width, 4, channels).transpose(1, 0, 2).reshape(-1, channels)
     taps = conv_weight[0].transpose(0, 2, 1).reshape(3 * inner, channels)
     top, weights, hidden, slope, active, bend = forward_tower(
-        bases, stem, taps, proj_weight[0], sections, unit
+        bases, stem_weight, taps, proj_weight[0], sections, unit
     )
     head_part, cot = head(top, targets, head_weight, factor)
     cot = cot.reshape(length, channels)

time: 136 us -> 131 us (0.963)
  Pallas kernels: 132 us -> 129 us
  local copies, waits for them, and re-layouts: 3.27 us -> 1.38 us
    pallas_call x1, Pallas kernels: 70.1 us -> 67.4 us  [backward_tower(): pl.pallas_call(kernel, out_shape=[jax.ShapeDtypeStruct((rows, channels),...]
    reshape x2 -> x0, local copies, waits for them, and re-layouts: 1.88 us -> none  [paired_body(): stem_weight.reshape(bin_width, 4, channels).transpose(1, 0, 2)]
where the time goes in v2:
time: 131 us
  Pallas kernels  129 us (98%)
  local copies, waits for them, and re-layouts  1.38 us (1%)
    pallas_call x1, Pallas kernels, backward_tower(): pl.pallas_call(kernel, out_shape=[jax.ShapeDtypeStruct((rows, channels),...  67.4 us
    pallas_call x1, Pallas kernels, forward_tower(): pl.pallas_call(kernel, out_shape=[jax.ShapeDtypeStruct((seqs, half, chann...  45.8 us
    pallas_call x1, Pallas kernels, head(): pl.pallas_call(kernel, out_shape=[jax.ShapeDtypeStruct((channels, tracks)...  13.9 us

profile of v2, /device:TPU:0, one launch (start us, length us, event | category | flops | bytes accessed | tf_op | source)
XLA Modules:
  0.0 130.9 jit_solution(11185139724570023946)
XLA Ops:
  0.6 0.0 copy-start.2
  0.6 45.8 %forward_tower.1 = (bf16[2,1536,384]{2,1,0:T(8,128)(2,1)}, bf16[4,768,384]{2,1,0:T(8,128)(2,1)}, bf16[3072,384]{1,0:T(8,128)(2,1)}, bf16[3072,384]{1,0:T(8,128)(...) custom-call(s32[2,1536,128]{2,1,0:T(8,128)} %refs_0_.1, ...), custom_call_target="tpu_custom_call" | custom-call | tf_op jit(solution)/shard_map/forward_tower/pallas_call | solution.py:279
  46.5 0.0 copy-done.2
  46.5 0.0 copy-start.1
  46.5 13.9 %head.1 = (f32[384,1024]{1,0:T(8,128)S(1)}, bf16[2,1536,384]{2,1,0:T(8,128)(2,1)S(1)}) custom-call(bf16[2,1536,384]{2,1,0:T(8,128)(2,1)} %get-tuple-element.27.top_ref, s32[2,1536,1024]{2,1,0:T(8,128)} %targets_ref.1, bf16[384,1024]{1,0:T(8,128)(2,1)S(1)} %copy-done.2), custom_call_target="tpu_custom_call" | custom-call | tf_op jit(solution)/shard_map/head/pallas_call | solution.py:373
  60.4 0.0 copy-start
  60.4 1.4 %copy-done = bf16[2,1536,384]{2,1,0:T(8,128)(2,1)} copy-done((bf16[2,1536,384]{2,1,0:T(8,128)(2,1)}, bf16[2,1536,384]{2,1,0:T(8,128)(2,1)S(1)}, u32[]{:S(2)}) %copy-start) | copy-done | bytes 2359320
  61.8 0.0 copy-done.1
  61.8 67.4 %backward_tower.1 = (f32[768,384]{1,0:T(8,128)S(1)}, f32[384,1024]{1,0:T(8,128)S(1)}) custom-call(f32[384,1024]{1,0:T(8,128)S(1)} %get-tuple-element.28.refs_0_, bf16[3072,384]{1,0:T(8,128)(2,1)} %bitcast.13, bf16[4,768,384]{2,1,0:T(8,128)(2,1)} %get-tuple-element.30.refs_2_, bf16[3072,384]{1,0:T(8,128)(2,1)} %get-tuple-element.31.refs_3_, ...), custom_call_target="tpu_custom_call" | custom-call | tf_op jit(solution)/shard_map/backward_tower/pallas_call | solution.py:795
  129.1 1.6 %finish.1 = (f32[576,384]{1,0:T(8,128)}, f32[192,384]{1,0:T(8,128)}, f32[384,1024]{1,0:T(8,128)}) custom-call(f32[768,384]{1,0:T(8,128)S(1)} %get-tuple-element.46.total_ref, f32[384,1024]{1,0:T(8,128)S(1)} %get-tuple-element.47.head_ref), custom_call_target="tpu_custom_call" | custom-call | tf_op jit(solution)/shard_map/finish/pallas_call | solution.py:856
Async XLA Ops:
  0.6 45.8 %copy-start.2 = (bf16[384,1024]{1,0:T(8,128)(2,1)S(1)}, bf16[384,1024]{1,0:T(8,128)(2,1)}, u32[]{:S(2)}) copy-start(bf16[384,1024]{1,0:T(8,128)(2,1)} %weight_ref.1) | copy-start | bytes 2359300
  46.5 15.3 %copy-start.1 = (bf16[3072,192]{1,0:T(8,128)(2,1)S(1)}, bf16[3072,192]{1,0:T(8,128)(2,1)}, u32[]{:S(2)}) copy-start(bf16[3072,192]{1,0:T(8,128)(2,1)} %get-tuple-element.38.refs_10_) | copy-start | bytes 3538948
  60.4 1.4 %copy-start = (bf16[2,1536,384]{2,1,0:T(8,128)(2,1)}, bf16[2,1536,384]{2,1,0:T(8,128)(2,1)S(1)}, u32[]{:S(2)}) copy-start(bf16[2,1536,384]{2,1,0:T(8,128)(2,1)S(1)} %get-tuple-element.29) | copy-start | bytes 7077892

commit v3 on v2

--- a/solution.py
+++ b/solution.py
@@ -713,7 +713,7 @@
                     marks.setdefault(at, []).append(stages[name].pop(0))
 
         for k in range(sections):
-            plan(k, [3 * (top - k) + 2 + gap for gap in (0, 2, 3, 6, 9)])
+            plan(k, [3 * (top - k) + 2 + gap for gap in (0, 2, 3, 6)])
         plan("h", (1, 5, 10))
         clock = [0]
 

time: 131 us -> 130 us (level)
  no operation moved by 1% of the time
where the time goes in v3:
time: 130 us
  Pallas kernels  128 us (98%)
  local copies, waits for them, and re-layouts  1.38 us (1%)
    pallas_call x1, Pallas kernels, backward_tower(): pl.pallas_call(kernel, out_shape=[jax.ShapeDtypeStruct((rows, channels),...  66.3 us
    pallas_call x1, Pallas kernels, forward_tower(): pl.pallas_call(kernel, out_shape=[jax.ShapeDtypeStruct((seqs, half, chann...  45.8 us
    pallas_call x1, Pallas kernels, head(): pl.pallas_call(kernel, out_shape=[jax.ShapeDtypeStruct((channels, tracks)...  13.9 us

profile of v3, /device:TPU:0, one launch (start us, length us, event | category | flops | bytes accessed | tf_op | source)
XLA Modules:
  0.0 129.8 jit_solution(10596816623940138663)
XLA Ops:
  0.6 0.0 copy-start.2
  0.6 45.8 %forward_tower.1 = (bf16[2,1536,384]{2,1,0:T(8,128)(2,1)}, bf16[4,768,384]{2,1,0:T(8,128)(2,1)}, bf16[3072,384]{1,0:T(8,128)(2,1)}, bf16[3072,384]{1,0:T(8,128)(...) custom-call(s32[2,1536,128]{2,1,0:T(8,128)} %refs_0_.1, ...), custom_call_target="tpu_custom_call" | custom-call | tf_op jit(solution)/shard_map/forward_tower/pallas_call | solution.py:279
  46.5 0.0 copy-done.2
  46.5 0.0 copy-start.1
  46.5 13.9 %head.1 = (f32[384,1024]{1,0:T(8,128)S(1)}, bf16[2,1536,384]{2,1,0:T(8,128)(2,1)S(1)}) custom-call(bf16[2,1536,384]{2,1,0:T(8,128)(2,1)} %get-tuple-element.27.top_ref, s32[2,1536,1024]{2,1,0:T(8,128)} %targets_ref.1, bf16[384,1024]{1,0:T(8,128)(2,1)S(1)} %copy-done.2), custom_call_target="tpu_custom_call" | custom-call | tf_op jit(solution)/shard_map/head/pallas_call | solution.py:373
  60.4 0.0 copy-start
  60.4 1.4 %copy-done = bf16[2,1536,384]{2,1,0:T(8,128)(2,1)} copy-done((bf16[2,1536,384]{2,1,0:T(8,128)(2,1)}, bf16[2,1536,384]{2,1,0:T(8,128)(2,1)S(1)}, u32[]{:S(2)}) %copy-start) | copy-done | bytes 2359320
  61.8 0.0 copy-done.1
  61.8 66.3 %backward_tower.1 = (f32[768,384]{1,0:T(8,128)S(1)}, f32[384,1024]{1,0:T(8,128)S(1)}) custom-call(f32[384,1024]{1,0:T(8,128)S(1)} %get-tuple-element.28.refs_0_, bf16[3072,384]{1,0:T(8,128)(2,1)} %bitcast.13, bf16[4,768,384]{2,1,0:T(8,128)(2,1)} %get-tuple-element.30.refs_2_, bf16[3072,384]{1,0:T(8,128)(2,1)} %get-tuple-element.31.refs_3_, ...), custom_call_target="tpu_custom_call" | custom-call | tf_op jit(solution)/shard_map/backward_tower/pallas_call | solution.py:795
  128.0 1.6 %finish.1 = (f32[576,384]{1,0:T(8,128)}, f32[192,384]{1,0:T(8,128)}, f32[384,1024]{1,0:T(8,128)}) custom-call(f32[768,384]{1,0:T(8,128)S(1)} %get-tuple-element.46.total_ref, f32[384,1024]{1,0:T(8,128)S(1)} %get-tuple-element.47.head_ref), custom_call_target="tpu_custom_call" | custom-call | tf_op jit(solution)/shard_map/finish/pallas_call | solution.py:856
Async XLA Ops:
  0.6 45.8 %copy-start.2 = (bf16[384,1024]{1,0:T(8,128)(2,1)S(1)}, bf16[384,1024]{1,0:T(8,128)(2,1)}, u32[]{:S(2)}) copy-start(bf16[384,1024]{1,0:T(8,128)(2,1)} %weight_ref.1) | copy-start | bytes 2359300
  46.5 15.3 %copy-start.1 = (bf16[3072,192]{1,0:T(8,128)(2,1)S(1)}, bf16[3072,192]{1,0:T(8,128)(2,1)}, u32[]{:S(2)}) copy-start(bf16[3072,192]{1,0:T(8,128)(2,1)} %get-tuple-element.38.refs_10_) | copy-start | bytes 3538948
  60.4 1.4 %copy-start = (bf16[2,1536,384]{2,1,0:T(8,128)(2,1)}, bf16[2,1536,384]{2,1,0:T(8,128)(2,1)S(1)}, u32[]{:S(2)}) copy-start(bf16[2,1536,384]{2,1,0:T(8,128)(2,1)S(1)} %get-tuple-element.29) | copy-start | bytes 7077892

commit v4 on v3

--- a/solution.py
+++ b/solution.py
@@ -247,21 +247,27 @@
                 keep(slope[k], slope_out[k])
             else:
 
-                def finish_half(number):
+                def finish_half(number, store):
                     def step(i, carry):
                         places = spots(i, number * half)
                         for place, new in zip(places, group(places, 1 - number, 2)):
-                            state[pl.ds(place, tile), :] = new
+                            store(place, new)
                         return carry
 
                     lax.fori_loop(0, steps // team, step, 0)
 
-                finish_half(1 - c)
+                def away(place, new):
+                    state[pl.ds(place, tile), :] = new
+
+                def here(place, new):
+                    start = pl.multiple_of(place - c * half, 16)
+                    top_ref[c, pl.ds(start, tile), :] = new
+
+                finish_half(1 - c, away)
                 theirs = state.at[pl.ds(pl.multiple_of((1 - c) * half, 16), half)]
                 last = remote(theirs, top_ref.at[c], tsend, trecv, partner)
                 last.start()
-                finish_half(c)
-                top_ref[c] = state[pl.ds(pl.multiple_of(c * half, 16), half), :]
+                finish_half(c, here)
             keep(active[k], active_out[k])
             keep(bend[k], bend_out[k])
         for copy in outs:
@@ -726,8 +732,6 @@
             by = unit * 2**k
             slot = k % 2
             above = cot_ref if k == top else grad
-            if k:
-                prefetch(k - 1)
             for copy in bring[k][0]:
                 copy.wait()
 
@@ -746,6 +750,8 @@
                 tick()
             for copy in bring[k][1]:
                 copy.wait()
+            if k:
+                prefetch(k - 1)
 
             def outward(i, carry, k=k, by=by, slot=slot, above=above):
                 place = pl.multiple_of(i * tile, 16)

time: 130 us -> 130 us (level)
  no operation moved by 1% of the time
where the time goes in v4:
time: 130 us
  Pallas kernels  127 us (98%)
  local copies, waits for them, and re-layouts  1.38 us (1%)
    pallas_call x1, Pallas kernels, backward_tower(): pl.pallas_call(kernel, out_shape=[jax.ShapeDtypeStruct((rows, channels),...  66.1 us
    pallas_call x1, Pallas kernels, forward_tower(): pl.pallas_call(kernel, out_shape=[jax.ShapeDtypeStruct((seqs, half, chann...  45.8 us
    pallas_call x1, Pallas kernels, head(): pl.pallas_call(kernel, out_shape=[jax.ShapeDtypeStruct((channels, tracks)...  13.9 us

profile of v4, /device:TPU:0, one launch (start us, length us, event | category | flops | bytes accessed | tf_op | source)
XLA Modules:
  0.0 129.6 jit_solution(4034751155275006049)
XLA Ops:
  0.6 0.0 copy-start.2
  0.6 45.8 %forward_tower.1 = (bf16[2,1536,384]{2,1,0:T(8,128)(2,1)}, bf16[4,768,384]{2,1,0:T(8,128)(2,1)}, bf16[3072,384]{1,0:T(8,128)(2,1)}, bf16[3072,384]{1,0:T(8,128)(...) custom-call(s32[2,1536,128]{2,1,0:T(8,128)} %refs_0_.1, ...), custom_call_target="tpu_custom_call" | custom-call | tf_op jit(solution)/shard_map/forward_tower/pallas_call | solution.py:285
  46.5 0.0 copy-done.2
  46.5 0.0 copy-start.1
  46.5 13.9 %head.1 = (f32[384,1024]{1,0:T(8,128)S(1)}, bf16[2,1536,384]{2,1,0:T(8,128)(2,1)S(1)}) custom-call(bf16[2,1536,384]{2,1,0:T(8,128)(2,1)} %get-tuple-element.27.top_ref, s32[2,1536,1024]{2,1,0:T(8,128)} %targets_ref.1, bf16[384,1024]{1,0:T(8,128)(2,1)S(1)} %copy-done.2), custom_call_target="tpu_custom_call" | custom-call | tf_op jit(solution)/shard_map/head/pallas_call | solution.py:379
  60.4 0.0 copy-start
  60.4 1.4 %copy-done = bf16[2,1536,384]{2,1,0:T(8,128)(2,1)} copy-done((bf16[2,1536,384]{2,1,0:T(8,128)(2,1)}, bf16[2,1536,384]{2,1,0:T(8,128)(2,1)S(1)}, u32[]{:S(2)}) %copy-start) | copy-done | bytes 2359320
  61.8 0.0 copy-done.1
  61.8 66.1 %backward_tower.1 = (f32[768,384]{1,0:T(8,128)S(1)}, f32[384,1024]{1,0:T(8,128)S(1)}) custom-call(f32[384,1024]{1,0:T(8,128)S(1)} %get-tuple-element.28.refs_0_, bf16[3072,384]{1,0:T(8,128)(2,1)} %bitcast.13, bf16[4,768,384]{2,1,0:T(8,128)(2,1)} %get-tuple-element.30.refs_2_, bf16[3072,384]{1,0:T(8,128)(2,1)} %get-tuple-element.31.refs_3_, ...), custom_call_target="tpu_custom_call" | custom-call | tf_op jit(solution)/shard_map/backward_tower/pallas_call | solution.py:801
  127.9 1.6 %finish.1 = (f32[576,384]{1,0:T(8,128)}, f32[192,384]{1,0:T(8,128)}, f32[384,1024]{1,0:T(8,128)}) custom-call(f32[768,384]{1,0:T(8,128)S(1)} %get-tuple-element.46.total_ref, f32[384,1024]{1,0:T(8,128)S(1)} %get-tuple-element.47.head_ref), custom_call_target="tpu_custom_call" | custom-call | tf_op jit(solution)/shard_map/finish/pallas_call | solution.py:862
Async XLA Ops:
  0.6 45.8 %copy-start.2 = (bf16[384,1024]{1,0:T(8,128)(2,1)S(1)}, bf16[384,1024]{1,0:T(8,128)(2,1)}, u32[]{:S(2)}) copy-start(bf16[384,1024]{1,0:T(8,128)(2,1)} %weight_ref.1) | copy-start | bytes 2359300
  46.5 15.3 %copy-start.1 = (bf16[3072,192]{1,0:T(8,128)(2,1)S(1)}, bf16[3072,192]{1,0:T(8,128)(2,1)}, u32[]{:S(2)}) copy-start(bf16[3072,192]{1,0:T(8,128)(2,1)} %get-tuple-element.38.refs_10_) | copy-start | bytes 3538948
  60.4 1.4 %copy-start = (bf16[2,1536,384]{2,1,0:T(8,128)(2,1)}, bf16[2,1536,384]{2,1,0:T(8,128)(2,1)S(1)}, u32[]{:S(2)}) copy-start(bf16[2,1536,384]{2,1,0:T(8,128)(2,1)S(1)} %get-tuple-element.29) | copy-start | bytes 7077892
